TPU v7x, 512 devices: a whole 4x4x16 slice. The times are simulated.
512 devices in a mesh: gx: 32 (over x, z_lo, core), gy: 16 (over y, z_hi).
Axes of the slice: x: 4, y: 4, z: 16 (z_hi: 4, z_lo: 4; z = z_hi * 4 + z_lo), core: 2. Of those that a mesh axis runs over, the one named last changes fastest.
Arguments:
- state_field: float32 [128, 128, 2304], P('gx', 'gy'), may hold values from -6 to 6
- conv_first: float32 [3, 3, 36, 108], replicated, may hold values from -0.1875 to 0.1875
- conv_second: float32 [3, 3, 36, 108], replicated, may hold values from -0.1875 to 0.1875
- spec_real: float32 [32, 32, 36, 432], P('gx', 'gy'), may hold values from -12 to 12
- spec_imag: float32 [32, 32, 36, 432], P('gx', 'gy'), may hold values from -12 to 12
Outputs:
- layer_out: float32 [128, 128, 2304], P('gx', 'gy')
All inputs are finite; a program needn't handle non-finite values.
Results may differ from a plain program's by a relative error of at most 0.00007.
Values sent between devices are 32-bit elements; how exact they have to be, the bound alone decides.
A program may use at most 128 MiB of HBM per device.

v0:
```python
import jax
import jax.numpy as jnp
from jax import lax
from jax.sharding import PartitionSpec as P

C = 36
Z = 64
MX = 16
MY = 16
MZ = 12
highest = lax.Precision.HIGHEST
two_pi = 6.283185307179586


def with_halo(cells, sides, width):
    for axis, dim in sides:
        count = lax.axis_size(axis)
        ends = count - 1
        head = lax.slice_in_dim(cells, 0, width, axis=dim)
        tail = lax.slice_in_dim(cells, cells.shape[dim] - width, cells.shape[dim], axis=dim)
        cells = jnp.concatenate(
            [
                lax.ppermute(tail, axis, [(i, (i + 1) % count) for i in range(ends)]),
                cells,
                lax.ppermute(head, axis, [((i + 1) % count, i) for i in range(ends)]),
            ],
            axis=dim,
        )
    return cells


def matmul(left, right):
    return jnp.dot(left, right, precision=highest)


def kept_modes(mode_count, length):
    places = jnp.arange(2 * mode_count, dtype=jnp.int32)
    return jnp.where(places < mode_count, places, places + length - 2 * mode_count)


def angle_table(first_index, second_index, length):
    product = first_index[:, None] * second_index[None, :] % length
    angles = product.astype(jnp.float32) * (two_pi / length)
    return (jnp.cos(angles), jnp.sin(angles))


def convolve(extended, kernel, rows_out, cols_out):
    shaped = extended.reshape(rows_out + 2, cols_out + 2, C, Z)
    moved = jnp.transpose(shaped, (2, 0, 1, 3))
    padded = jnp.pad(moved, ((0, 0), (0, 0), (0, 0), (1, 1)))
    summed = jnp.zeros((C, rows_out * cols_out * Z), jnp.float32)
    for shift_x in range(3):
        for shift_y in range(3):
            for shift_z in range(3):
                window = padded[
                    :,
                    shift_x : shift_x + rows_out,
                    shift_y : shift_y + cols_out,
                    shift_z : shift_z + Z,
                ]
                block = kernel[shift_x, shift_y, :, shift_z * C : (shift_z + 1) * C]
                summed = summed + matmul(block, window.reshape(C, rows_out * cols_out * Z))
    return jnp.transpose(summed.reshape(C, rows_out, cols_out, Z), (1, 2, 0, 3))


def on_device(state_field, conv_first, conv_second, spec_real, spec_imag):
    rows_here = state_field.shape[0]
    cols_here = state_field.shape[1]
    total_x = rows_here * lax.axis_size("gx")
    total_y = cols_here * lax.axis_size("gy")
    row_start = lax.axis_index("gx") * rows_here
    col_start = lax.axis_index("gy") * cols_here
    chan_modes = C * MZ
    width_q = cols_here * chan_modes
    extended = with_halo(state_field, (("gx", 0), ("gy", 1)), 1)
    hidden_field = jax.nn.gelu(
        convolve(extended, conv_first, rows_here, cols_here), approximate=False
    )
    hidden_rim = with_halo(
        hidden_field.reshape(rows_here, cols_here, C * Z), (("gx", 0), ("gy", 1)), 1
    )
    conv_out = convolve(hidden_rim, conv_second, rows_here, cols_here)
    z_cells = jnp.arange(Z, dtype=jnp.int32)
    z_freqs = jnp.arange(MZ, dtype=jnp.int32)
    z_cosine, z_sine = angle_table(z_cells, z_freqs, Z)
    flat_cells = state_field.reshape(rows_here * cols_here * C, Z)
    z_real = matmul(flat_cells, z_cosine).reshape(rows_here, width_q)
    z_imag = -matmul(flat_cells, z_sine).reshape(rows_here, width_q)
    x_freqs = kept_modes(MX, total_x)
    local_x = row_start + jnp.arange(rows_here, dtype=jnp.int32)
    frequency = x_freqs
    cosine, sine_part = angle_table(frequency, local_x, total_x)
    term_real = matmul(cosine, z_real) + matmul(sine_part, z_imag)
    term_imag = matmul(cosine, z_imag) - matmul(sine_part, z_real)
    joined = lax.psum_scatter(
        jnp.concatenate([term_real, term_imag], axis=1), "gx", scatter_dimension=0, tiled=True
    )
    mode_real = joined[:, :width_q]
    mode_imag = joined[:, width_q:]
    kxd_rows = mode_real.shape[0]
    y_real = mode_real.reshape(kxd_rows, cols_here, chan_modes)
    y_imag = mode_imag.reshape(kxd_rows, cols_here, chan_modes)
    y_freqs = kept_modes(MY, total_y)
    local_y = col_start + jnp.arange(cols_here, dtype=jnp.int32)
    frequency = y_freqs
    cosine, sine_part = angle_table(frequency, local_y, total_y)
    term_real = jnp.einsum("my,ayq->maq", cosine, y_real, precision=highest) + jnp.einsum(
        "my,ayq->maq", sine_part, y_imag, precision=highest
    )
    term_imag = jnp.einsum("my,ayq->maq", cosine, y_imag, precision=highest) - jnp.einsum(
        "my,ayq->maq", sine_part, y_real, precision=highest
    )
    owned = lax.psum_scatter(
        jnp.concatenate([term_real, term_imag], axis=2), "gy", scatter_dimension=0, tiled=True
    )
    kyd_rows = owned.shape[0]
    owned_real = owned[..., :chan_modes].reshape(kyd_rows, kxd_rows, C, MZ)
    owned_imag = owned[..., chan_modes:].reshape(kyd_rows, kxd_rows, C, MZ)
    weight_real = spec_real.reshape(kxd_rows, kyd_rows, C, MZ, C)
    weight_imag = spec_imag.reshape(kxd_rows, kyd_rows, C, MZ, C)
    mixed_real = jnp.einsum(
        "baik,abiko->baok", owned_real, weight_real, precision=highest
    ) - jnp.einsum("baik,abiko->baok", owned_imag, weight_imag, precision=highest)
    mixed_imag = jnp.einsum(
        "baik,abiko->baok", owned_real, weight_imag, precision=highest
    ) + jnp.einsum("baik,abiko->baok", owned_imag, weight_real, precision=highest)
    mixed = jnp.concatenate(
        [
            mixed_real.reshape(kyd_rows, kxd_rows, chan_modes),
            mixed_imag.reshape(kyd_rows, kxd_rows, chan_modes),
        ],
        axis=2,
    )
    shard_piece = lax.all_gather(mixed, "gy", axis=0, tiled=True)
    frequency = y_freqs
    cosine, sine_part = angle_table(local_y, frequency, total_y)
    piece_real = shard_piece[..., :chan_modes]
    piece_imag = shard_piece[..., chan_modes:]
    add_real = jnp.einsum("ym,maq->ayq", cosine, piece_real, precision=highest) - jnp.einsum(
        "ym,maq->ayq", sine_part, piece_imag, precision=highest
    )
    add_imag = jnp.einsum("ym,maq->ayq", cosine, piece_imag, precision=highest) + jnp.einsum(
        "ym,maq->ayq", sine_part, piece_real, precision=highest
    )
    returned = jnp.concatenate([add_real, add_imag], axis=2)
    back_real = returned[..., :chan_modes].reshape(kxd_rows, width_q)
    back_imag = returned[..., chan_modes:].reshape(kxd_rows, width_q)
    joined_back = jnp.concatenate([back_real, back_imag], axis=1)
    shard_piece = lax.all_gather(joined_back, "gx", axis=0, tiled=True)
    frequency = x_freqs
    cosine, sine_part = angle_table(local_x, frequency, total_x)
    piece_real = shard_piece[:, :width_q]
    piece_imag = shard_piece[:, width_q:]
    add_real = matmul(cosine, piece_real) - matmul(sine_part, piece_imag)
    add_imag = matmul(cosine, piece_imag) + matmul(sine_part, piece_real)
    gathered = jnp.concatenate([add_real, add_imag], axis=1)
    cell_real = gathered[:, :width_q]
    cell_imag = gathered[:, width_q:]
    scaling = 1.0 / (total_x * total_y * Z)
    factors = jnp.where(z_freqs == 0, 1.0, 2.0).astype(jnp.float32) * scaling
    back_cosine, back_sine = angle_table(z_freqs, z_cells, Z)
    back_cosine = back_cosine * factors[:, None]
    back_sine = back_sine * factors[:, None]
    spectral = matmul(cell_real.reshape(rows_here * cols_here * C, MZ), back_cosine) - matmul(
        cell_imag.reshape(rows_here * cols_here * C, MZ), back_sine
    )
    spectral = spectral.reshape(rows_here, cols_here, C, Z)
    layer_out = jax.nn.gelu(spectral + conv_out, approximate=False)
    return layer_out.reshape(rows_here, cols_here, C * Z)


def solution(mesh):
    in_specs = (P("gx", "gy", None), P(), P(), P("gx", "gy", None, None), P("gx", "gy", None, None))
    out_specs = P("gx", "gy", None)
    return jax.shard_map(
        on_device, mesh=mesh, in_specs=in_specs, out_specs=out_specs, check_vma=False
    )
```

profile of v0, /device:TPU:1, one launch (start us, length us, event | category | flops | bytes accessed | tf_op | source)
XLA Modules:
  0.0 637.4 jit_solution(1770213632262422438)
XLA Ops:
  7.5 8.8 %collective-permute-start.1 = (f32[1,8,2304]{2,1,0:T(8,128)S(1)}, f32[1,8,2304]{2,1,0:T(8,128)S(1)}, u32[]{:S(2)}, u32[]{:S(2)}) collective-permute-start(f32[1,8,2304]{2,1,0:T(8,128)S(1)} %get-tuple-element.75), channel_id=1, source_target_pairs={{16,0},{32,16},{48,32},{64,48},{80,64},{96,80},{112,96},{128,112},... | collective-permute-start | bytes 221192 | tf_op jit(solution)/shard_map/ppermute | solution.py:25
  24.9 5.0 collective-permute-start.2
  32.8 10.6 %collective-permute-done.3 = f32[6,1,2304]{2,1,0:T(1,128)S(1)} collective-permute-done((f32[6,1,2304]{2,1,0:T(1,128)S(1)}, f32[6,1,2304]{2,1,0:T(1,128)S(1)}, u32[]{:S(2)}, u32[]{:S(2)}) %collective-permute-start.3) | collective-permute-done | bytes 55328 | tf_op jit(solution)/shard_map/ppermute | solution.py:25
  46.2 4.3 pad_slice_fusion.24
  50.5 3.8 fusion.326
  75.8 2.0 reshape.340
  85.3 2.0 reshape.344
  94.8 2.0 reshape.349
  101.5 2.1 fusion.130
  103.6 2.2 convolution_bitcast_fusion.11
  107.0 2.0 reshape.354
  110.1 2.0 reshape.352
  113.3 2.0 reshape.353
  121.0 2.2 convolution_bitcast_fusion.16
  124.5 2.1 convolution_bitcast_fusion.15
  127.9 2.2 convolution_bitcast_fusion.13
  151.6 2.4 collective-permute-start.5
  154.1 3.6 collective-permute-done.5
  157.8 8.5 %collective-permute-start.6 = (f32[6,1,2304]{2,1,0:T(1,128)S(1)}, f32[6,1,2304]{2,1,0:T(1,128)S(1)}, u32[]{:S(2)}, u32[]{:S(2)}) collective-permute-start(f32[6,1,2304]{2,1,0:T(1,128)S(1)} %get-tuple-element.69), channel_id=1, source_target_pairs={{0,1},{1,2},{2,3},{3,4},{4,5},{5,6},{6,7},{7,8},{8,9},{9,10},{10,1... | collective-permute-start | bytes 165896 | tf_op jit(solution)/shard_map/ppermute | solution.py:23
  173.5 4.0 collective-permute-done.7
  180.4 4.3 pad_slice_fusion.6
  184.6 3.8 fusion.324
  200.4 2.0 reshape.368
  210.0 2.0 reshape.369
  213.2 2.0 reshape.370
  216.3 2.0 reshape.372
  236.9 2.1 fusion.102
  241.4 2.0 reshape.383
  280.7 38.4 %all-reduce.7.cloned.1.call-done = f32[32,6912]{1,0:T(8,128)} async-done(((f32[32,6912]{1,0:T(8,128)}), f32[32,6912]{1,0:T(8,128)}) %all-reduce.7.cloned.1.call-update) | async-done | bytes 884752
  325.2 188.3 %all-reduce.9.cloned.1.call-done = f32[32,1,864]{2,0,1:T(8,128)} async-done(((f32[32,1,864]{2,0,1:T(8,128)}), f32[32,1,864]{2,0,1:T(8,128)}) %all-reduce.9.cloned.1.call-update) | async-done | bytes 110608
  515.8 42.2 %all_gather.6 = f32[32,1,864]{2,1,0:T(1,128)S(1)} all-gather(f32[2,1,864]{2,1,0:T(1,128)S(1)} %copy.74), channel_id=1, replica_groups=mesh['gx'=32,'gy'=16] {'gy'}, dimensions={0}, use_global_device_ids=true | all-gather | bytes 117504 | tf_op jit(solution)/shard_map/all_gather | solution.py:134
  559.5 63.2 %all-gather = f32[32,1,6912]{2,1,0:T(1,128)S(1)} all-gather(f32[1,1,6912]{2,1,0:T(1,128)S(1)} %maximum_bitcast_fusion), channel_id=1, replica_groups=mesh['gx'=32,'gy'=16] {'gx'}, dimensions={0}, use_global_device_ids=true | all-gather | bytes 912384 | tf_op jit(solution)/shard_map/all_gather | solution.py:149
  (452 shorter events, 195.4 us)
Async XLA Ops:
  6.5 312.6 %all-reduce.7.cloned.1.call-start = ((), (), s32[]{:S(2)}) async-start(), calls=%async_computation | async-start | bytes 1769472
  7.5 17.3 %collective-permute-start.1 = (f32[1,8,2304]{2,1,0:T(8,128)S(1)}, f32[1,8,2304]{2,1,0:T(8,128)S(1)}, u32[]{:S(2)}, u32[]{:S(2)}) collective-permute-start(f32[1,8,2304]{2,1,0:T(8,128)S(1)} %get-tuple-element.75), channel_id=1, source_target_pairs={{16,0},{32,16},{48,32},{64,48},{80,64},{96,80},{112,96},{128,112},... | collective-permute-start | bytes 221192 | tf_op jit(solution)/shard_map/ppermute | solution.py:25
  16.3 8.5 %collective-permute-start = (f32[1,8,2304]{2,1,0:T(8,128)S(1)}, f32[1,8,2304]{2,1,0:T(8,128)S(1)}, u32[]{:S(2)}, u32[]{:S(2)}) collective-permute-start(f32[1,8,2304]{2,1,0:T(8,128)S(1)} %get-tuple-element.76), channel_id=1, source_target_pairs={{0,16},{16,32},{32,48},{48,64},{64,80},{80,96},{96,112},{112,128},... | collective-permute-start | bytes 221192 | tf_op jit(solution)/shard_map/ppermute | solution.py:23
  24.9 7.9 %collective-permute-start.2 = (f32[6,1,2304]{2,1,0:T(1,128)S(1)}, f32[6,1,2304]{2,1,0:T(1,128)S(1)}, u32[]{:S(2)}, u32[]{:S(2)}) collective-permute-start(f32[6,1,2304]{2,1,0:T(1,128)S(1)} %get-tuple-element.71), channel_id=1, source_target_pairs={{0,1},{1,2},{2,3},{3,4},{4,5},{5,6},{6,7},{7,8},{8,9},{9,10},{10,1... | collective-permute-start | bytes 165896 | tf_op jit(solution)/shard_map/ppermute | solution.py:23
  29.9 13.5 %collective-permute-start.3 = (f32[6,1,2304]{2,1,0:T(1,128)S(1)}, f32[6,1,2304]{2,1,0:T(1,128)S(1)}, u32[]{:S(2)}, u32[]{:S(2)}) collective-permute-start(f32[6,1,2304]{2,1,0:T(1,128)S(1)} %get-tuple-element.72), channel_id=1, source_target_pairs={{1,0},{2,1},{3,2},{4,3},{5,4},{6,5},{7,6},{8,7},{9,8},{10,9},{11,1... | collective-permute-start | bytes 165896 | tf_op jit(solution)/shard_map/ppermute | solution.py:25
  32.2 481.3 %all-reduce.9.cloned.1.call-start = ((), (), s32[]{:S(2)}) async-start(), calls=%async_computation.1 | async-start | bytes 229376
  96.8 3.3 copy-start.16
  100.5 5.3 copy-start.14
  116.5 3.2 copy-start.6
  149.3 21.2 %copy-start.100 = (f32[1,2,36,432]{3,1,2,0:T(2,128)S(1)}, f32[1,2,36,432]{3,1,2,0:T(2,128)}, u32[]{:S(2)}) copy-start(f32[1,2,36,432]{3,1,2,0:T(2,128)} %param.8) | copy-start | bytes 373252
  149.4 4.6 collective-permute-start.4
  151.5 20.2 %copy-start.101 = (f32[1,2,36,432]{3,1,2,0:T(2,128)S(1)}, f32[1,2,36,432]{3,1,2,0:T(2,128)}, u32[]{:S(2)}) copy-start(f32[1,2,36,432]{3,1,2,0:T(2,128)} %param.9) | copy-start | bytes 373252
  151.6 6.1 collective-permute-start.5
  157.8 15.7 %collective-permute-start.6 = (f32[6,1,2304]{2,1,0:T(1,128)S(1)}, f32[6,1,2304]{2,1,0:T(1,128)S(1)}, u32[]{:S(2)}, u32[]{:S(2)}) collective-permute-start(f32[6,1,2304]{2,1,0:T(1,128)S(1)} %get-tuple-element.69), channel_id=1, source_target_pairs={{0,1},{1,2},{2,3},{3,4},{4,5},{5,6},{6,7},{7,8},{8,9},{9,10},{10,1... | collective-permute-start | bytes 165896 | tf_op jit(solution)/shard_map/ppermute | solution.py:23
  166.3 11.2 %collective-permute-start.7 = (f32[6,1,2304]{2,1,0:T(1,128)S(1)}, f32[6,1,2304]{2,1,0:T(1,128)S(1)}, u32[]{:S(2)}, u32[]{:S(2)}) collective-permute-start(f32[6,1,2304]{2,1,0:T(1,128)S(1)} %get-tuple-element.70), channel_id=1, source_target_pairs={{1,0},{2,1},{3,2},{4,3},{5,4},{6,5},{7,6},{8,7},{9,8},{10,9},{11,1... | collective-permute-start | bytes 165896 | tf_op jit(solution)/shard_map/ppermute | solution.py:25
  227.8 3.3 copy-start.19
  235.5 4.7 copy-start.15
  240.2 3.2 copy-start.13
  249.7 3.6 copy-start.7
  253.4 3.7 copy-start.5
  257.0 3.6 copy-start.3
  260.7 3.6 copy-start.1
  279.0 44.1 %copy-start.58 = (f32[36,2048]{1,0:T(8,128)S(1)}, f32[36,2048]{1,0:T(8,128)}, u32[]{:S(2)}) copy-start(f32[36,2048]{1,0:T(8,128)} %convolution_bitcast_fusion.3) | copy-start | bytes 884740
  279.0 44.1 %copy-start.59 = (f32[36,2048]{1,0:T(8,128)S(1)}, f32[36,2048]{1,0:T(8,128)}, u32[]{:S(2)}) copy-start(f32[36,2048]{1,0:T(8,128)} %convolution_bitcast_fusion.2) | copy-start | bytes 884740
  279.0 44.1 %copy-start.60 = (f32[36,2048]{1,0:T(8,128)S(1)}, f32[36,2048]{1,0:T(8,128)}, u32[]{:S(2)}) copy-start(f32[36,2048]{1,0:T(8,128)} %convolution_bitcast_fusion) | copy-start | bytes 884740
  279.4 43.7 %copy-start.51 = (f32[36,2048]{1,0:T(8,128)S(1)}, f32[36,2048]{1,0:T(8,128)}, u32[]{:S(2)}) copy-start(f32[36,2048]{1,0:T(8,128)} %reshape.384) | copy-start | bytes 884740
  279.4 43.7 %copy-start.53 = (f32[36,2048]{1,0:T(8,128)S(1)}, f32[36,2048]{1,0:T(8,128)}, u32[]{:S(2)}) copy-start(f32[36,2048]{1,0:T(8,128)} %convolution_bitcast_fusion.1) | copy-start | bytes 884740
  279.5 43.7 %copy-start.54 = (f32[36,2048]{1,0:T(8,128)S(1)}, f32[36,2048]{1,0:T(8,128)}, u32[]{:S(2)}) copy-start(f32[36,2048]{1,0:T(8,128)} %convolution_bitcast_fusion.8) | copy-start | bytes 884740
  279.5 43.7 %copy-start.55 = (f32[36,2048]{1,0:T(8,128)S(1)}, f32[36,2048]{1,0:T(8,128)}, u32[]{:S(2)}) copy-start(f32[36,2048]{1,0:T(8,128)} %convolution_bitcast_fusion.6) | copy-start | bytes 884740
  279.5 43.7 %copy-start.56 = (f32[36,2048]{1,0:T(8,128)S(1)}, f32[36,2048]{1,0:T(8,128)}, u32[]{:S(2)}) copy-start(f32[36,2048]{1,0:T(8,128)} %convolution_bitcast_fusion.5) | copy-start | bytes 884740
  324.9 189.7 %copy-start.46 = (f32[2,36,12,36]{3,2,0,1:T(8,128)S(1)}, f32[2,36,12,36]{3,2,0,1:T(8,128)}, u32[]{:S(2)}) copy-start(f32[2,36,12,36]{3,2,0,1:T(8,128)} %reshape.325) | copy-start | bytes 373252
  324.9 189.7 %copy-start.47 = (f32[2,36,12,36]{3,2,0,1:T(8,128)S(1)}, f32[2,36,12,36]{3,2,0,1:T(8,128)}, u32[]{:S(2)}) copy-start(f32[2,36,12,36]{3,2,0,1:T(8,128)} %reshape.327) | copy-start | bytes 373252
  (80 other events, 167.6 us)
Sparse Core Ops, SparseCore 0:
  32.3 286.7 all-reduce.6
  323.2 190.2 all-reduce.8
where the time goes:
time: 644 us; the launch traced here: 637 us
  waiting for transfers between devices  245 us (38%)
  local copies, waits for them, and re-layouts  174 us (27%)
  blocking collectives  105 us (16%)
  matrix products  58.9 us (9%)
  starting transfers between devices  32 us (5%)
  between operations  15.8 us (2%)
    unnamed x4, waiting for transfers between devices  227 us
    reshape x54, local copies, waits for them, and re-layouts, convolve(): summed = summed + matmul(block, window.reshape(C, rows_out * cols_out * Z))  82.9 us
    slice x60, local copies, waits for them, and re-layouts, convolve(): padded[:, shift_x:shift_x + rows_out, shift_y:shift_y + cols_out, shift_z...  72 us
    all_gather x1, blocking collectives, on_device(): shard_piece = lax.all_gather(joined_back, 'gx', axis=0, tiled=True)  63.2 us
    dot_general x66, matrix products, matmul(): return jnp.dot(left, right, precision=highest)  56.6 us
    all_gather x1, blocking collectives, on_device(): shard_piece = lax.all_gather(mixed, 'gy', axis=0, tiled=True)  42.2 us
    ppermute x4, waiting for transfers between devices, with_halo(): lax.ppermute(head, axis, [((i + 1) % count, i) for i in range(ends)])  18.2 us
    ppermute x4, starting transfers between devices, with_halo(): lax.ppermute(tail, axis, [(i, (i + 1) % count) for i in range(ends)])  17.3 us
  transfers between devices with their start and end apart: 10, of which 5 were waited for; matrix products, arithmetic and copies ran while one was open for 35% of the time, Pallas kernels for 0%

commit v1 on v0

--- a/solution.py
+++ b/solution.py
@@ -10,6 +10,11 @@
 MZ = 12
 highest = lax.Precision.HIGHEST
 two_pi = 6.283185307179586
+
+
+def exchange_gather(value, axis, along):
+    sent = jnp.stack([value] * lax.axis_size(axis))
+    return jnp.concatenate(lax.all_to_all(sent, axis, 0, 0), axis=along)
 
 
 def with_halo(cells, sides, width):
@@ -131,7 +136,7 @@
         ],
         axis=2,
     )
-    shard_piece = lax.all_gather(mixed, "gy", axis=0, tiled=True)
+    shard_piece = exchange_gather(mixed, "gy", 0)
     frequency = y_freqs
     cosine, sine_part = angle_table(local_y, frequency, total_y)
     piece_real = shard_piece[..., :chan_modes]

time: 644 us -> 619 us (0.961)
  blocking collectives: 105 us -> 59.2 us
  local copies, waits for them, and re-layouts: 174 us -> 213 us
  waiting for transfers between devices: 245 us -> 216 us
  starting transfers between devices: 32 us -> 39 us
    all_gather x1 -> x0, blocking collectives: 42.2 us -> none  [on_device(): shard_piece = lax.all_gather(mixed, 'gy', axis=0, tiled=True)]
    unnamed x4, waiting for transfers between devices: 227 us -> 188 us
    slice x60, local copies, waits for them, and re-layouts: 72 us -> 99.4 us  [convolve(): padded[:, shift_x:shift_x + rows_out, shift_y:shift_y + cols_out, shift_z...]
    reshape x54, local copies, waits for them, and re-layouts: 82.9 us -> 93.2 us  [convolve(): summed = summed + matmul(block, window.reshape(C, rows_out * cols_out * Z))]
    all_to_all x0 -> x1, waiting for transfers between devices: none -> 9.42 us  [exchange_gather(): return jnp.concatenate(lax.all_to_all(sent, axis, 0, 0), axis=along)]
    all_to_all x0 -> x1, starting transfers between devices: none -> 7.1 us  [exchange_gather(): return jnp.concatenate(lax.all_to_all(sent, axis, 0, 0), axis=along)]
  transfers between devices with their start and end apart: 10 -> 11, of which waited for: 5 -> 5; matrix products, arithmetic and copies ran while one was open for 35% -> 43% of each run, Pallas kernels for 0% -> 0%
where the time goes in v1:
time: 619 us; the launch traced here: 612 us
  waiting for transfers between devices  216 us (35%)
  local copies, waits for them, and re-layouts  213 us (34%)
  matrix products  63.8 us (10%)
  blocking collectives  59.2 us (10%)
  starting transfers between devices  39 us (6%)
  between operations  15.5 us (3%)
    unnamed x4, waiting for transfers between devices  188 us
    slice x60, local copies, waits for them, and re-layouts, convolve(): padded[:, shift_x:shift_x + rows_out, shift_y:shift_y + cols_out, shift_z...  99.4 us
    reshape x54, local copies, waits for them, and re-layouts, convolve(): summed = summed + matmul(block, window.reshape(C, rows_out * cols_out * Z))  93.2 us
    dot_general x66, matrix products, matmul(): return jnp.dot(left, right, precision=highest)  61.5 us
    all_gather x1, blocking collectives, on_device(): shard_piece = lax.all_gather(joined_back, 'gx', axis=0, tiled=True)  59.2 us
    ppermute x4, waiting for transfers between devices, with_halo(): lax.ppermute(head, axis, [((i + 1) % count, i) for i in range(ends)])  18.1 us
    ppermute x4, starting transfers between devices, with_halo(): lax.ppermute(tail, axis, [(i, (i + 1) % count) for i in range(ends)])  17.1 us
    ppermute x4, starting transfers between devices, with_halo(): lax.ppermute(head, axis, [((i + 1) % count, i) for i in range(ends)])  14.2 us
  transfers between devices with their start and end apart: 11, of which 5 were waited for; matrix products, arithmetic and copies ran while one was open for 43% of the time, Pallas kernels for 0%

profile of v1, /device:TPU:1, one launch (start us, length us, event | category | flops | bytes accessed | tf_op | source)
XLA Modules:
  0.0 611.7 jit_solution(13462743795642839042)
XLA Ops:
  7.5 8.8 %collective-permute-start.1 = (f32[1,8,2304]{2,1,0:T(8,128)S(1)}, f32[1,8,2304]{2,1,0:T(8,128)S(1)}, u32[]{:S(2)}, u32[]{:S(2)}) collective-permute-start(f32[1,8,2304]{2,1,0:T(8,128)S(1)} %get-tuple-element.75), channel_id=1, source_target_pairs={{16,0},{32,16},{48,32},{64,48},{80,64},{96,80},{112,96},{128,112},... | collective-permute-start | bytes 221192 | tf_op jit(solution)/shard_map/ppermute | solution.py:30
  24.9 5.0 collective-permute-start.2
  32.8 10.6 %collective-permute-done.3 = f32[6,1,2304]{2,1,0:T(1,128)S(1)} collective-permute-done((f32[6,1,2304]{2,1,0:T(1,128)S(1)}, f32[6,1,2304]{2,1,0:T(1,128)S(1)}, u32[]{:S(2)}, u32[]{:S(2)}) %collective-permute-start.3) | collective-permute-done | bytes 55328 | tf_op jit(solution)/shard_map/ppermute | solution.py:30
  46.2 4.2 pad_slice_fusion.24
  50.5 3.9 fusion.326
  60.7 2.3 copy.83
  68.2 2.3 copy.77
  75.0 2.3 copy.93
  89.2 2.3 copy.82
  96.6 2.3 copy.85
  104.1 2.3 copy.88
  119.1 2.3 copy.91
  171.1 2.4 collective-permute-start.5
  173.6 3.7 collective-permute-done.5
  177.4 8.3 %collective-permute-start.6 = (f32[6,1,2304]{2,1,0:T(1,128)S(1)}, f32[6,1,2304]{2,1,0:T(1,128)S(1)}, u32[]{:S(2)}, u32[]{:S(2)}) collective-permute-start(f32[6,1,2304]{2,1,0:T(1,128)S(1)} %get-tuple-element.69), channel_id=1, source_target_pairs={{0,1},{1,2},{2,3},{3,4},{4,5},{5,6},{6,7},{7,8},{8,9},{9,10},{10,1... | collective-permute-start | bytes 165896 | tf_op jit(solution)/shard_map/ppermute | solution.py:28
  192.9 3.7 collective-permute-done.7
  199.5 4.1 pad_slice_fusion.6
  203.6 4.0 fusion.324
  208.2 2.3 copy.116
  215.7 2.3 copy.110
  223.2 2.3 copy.106
  230.7 2.3 copy.109
  238.2 2.4 copy.112
  245.7 2.3 copy.115
  253.3 2.3 copy.118
  268.6 2.4 copy.120
  276.1 2.3 copy.124
  296.2 2.3 copy.130
  324.0 188.0 %all-reduce.9.cloned.1.call-done = f32[32,1,864]{2,0,1:T(8,128)} async-done(((f32[32,1,864]{2,0,1:T(8,128)}), f32[32,1,864]{2,0,1:T(8,128)}) %all-reduce.9.cloned.1.call-update) | async-done | bytes 110608
  515.0 7.1 %all-to-all-start = ((f32[16,2,1,864]{3,2,1,0:T(1,128)}), f32[16,2,1,864]{3,2,1,0:T(1,128)S(1)}, u32[]{:S(2)}, u32[]{:S(2)}) async-start(f32[16,2,1,864]{3,2,1,0:T(1,128)} %stack.2), calls=%async_computation | async-start | bytes 229376 | tf_op jit(solution)/shard_map/all_to_all | solution.py:17
  526.9 9.4 %all-to-all-done = f32[16,2,1,864]{3,2,1,0:T(1,128)S(1)} async-done(((f32[16,2,1,864]{3,2,1,0:T(1,128)}), f32[16,2,1,864]{3,2,1,0:T(1,128)S(1)}, u32[]{:S(2)}, u32[]{:S(2)}) %all-to-all-start) | async-done | bytes 110624 | tf_op jit(solution)/shard_map/all_to_all | solution.py:17
  537.8 59.2 %all-gather = f32[32,1,6912]{2,1,0:T(1,128)S(1)} all-gather(f32[1,1,6912]{2,1,0:T(1,128)S(1)} %maximum_bitcast_fusion), channel_id=1, replica_groups=mesh['gx'=32,'gy'=16] {'gx'}, dimensions={0}, use_global_device_ids=true | all-gather | bytes 912384 | tf_op jit(solution)/shard_map/all_gather | solution.py:154
  (401 shorter events, 234.1 us)
Async XLA Ops:
  6.5 311.7 %all-reduce.7.cloned.1.call-start = ((), (), s32[]{:S(2)}) async-start(), calls=%async_computation.1 | async-start | bytes 1769472
  7.5 17.3 %collective-permute-start.1 = (f32[1,8,2304]{2,1,0:T(8,128)S(1)}, f32[1,8,2304]{2,1,0:T(8,128)S(1)}, u32[]{:S(2)}, u32[]{:S(2)}) collective-permute-start(f32[1,8,2304]{2,1,0:T(8,128)S(1)} %get-tuple-element.75), channel_id=1, source_target_pairs={{16,0},{32,16},{48,32},{64,48},{80,64},{96,80},{112,96},{128,112},... | collective-permute-start | bytes 221192 | tf_op jit(solution)/shard_map/ppermute | solution.py:30
  16.3 8.5 %collective-permute-start = (f32[1,8,2304]{2,1,0:T(8,128)S(1)}, f32[1,8,2304]{2,1,0:T(8,128)S(1)}, u32[]{:S(2)}, u32[]{:S(2)}) collective-permute-start(f32[1,8,2304]{2,1,0:T(8,128)S(1)} %get-tuple-element.76), channel_id=1, source_target_pairs={{0,16},{16,32},{32,48},{48,64},{64,80},{80,96},{96,112},{112,128},... | collective-permute-start | bytes 221192 | tf_op jit(solution)/shard_map/ppermute | solution.py:28
  24.9 7.9 %collective-permute-start.2 = (f32[6,1,2304]{2,1,0:T(1,128)S(1)}, f32[6,1,2304]{2,1,0:T(1,128)S(1)}, u32[]{:S(2)}, u32[]{:S(2)}) collective-permute-start(f32[6,1,2304]{2,1,0:T(1,128)S(1)} %get-tuple-element.71), channel_id=1, source_target_pairs={{0,1},{1,2},{2,3},{3,4},{4,5},{5,6},{6,7},{7,8},{8,9},{9,10},{10,1... | collective-permute-start | bytes 165896 | tf_op jit(solution)/shard_map/ppermute | solution.py:28
  29.9 13.5 %collective-permute-start.3 = (f32[6,1,2304]{2,1,0:T(1,128)S(1)}, f32[6,1,2304]{2,1,0:T(1,128)S(1)}, u32[]{:S(2)}, u32[]{:S(2)}) collective-permute-start(f32[6,1,2304]{2,1,0:T(1,128)S(1)} %get-tuple-element.72), channel_id=1, source_target_pairs={{1,0},{2,1},{3,2},{4,3},{5,4},{6,5},{7,6},{8,7},{9,8},{10,9},{11,1... | collective-permute-start | bytes 165896 | tf_op jit(solution)/shard_map/ppermute | solution.py:30
  32.2 479.8 %all-reduce.9.cloned.1.call-start = ((), (), s32[]{:S(2)}) async-start(), calls=%async_computation.2 | async-start | bytes 229376
  60.7 4.3 copy-start.24
  68.2 4.3 copy-start.22
  89.1 4.3 copy-start.16
  96.6 4.3 copy-start.14
  104.1 4.5 copy-start.12
  168.8 21.2 %copy-start.74 = (f32[1,2,36,432]{3,1,2,0:T(2,128)S(1)}, f32[1,2,36,432]{3,1,2,0:T(2,128)}, u32[]{:S(2)}) copy-start(f32[1,2,36,432]{3,1,2,0:T(2,128)} %param.8) | copy-start | bytes 373252
  168.9 4.6 collective-permute-start.4
  171.0 20.2 %copy-start.75 = (f32[1,2,36,432]{3,1,2,0:T(2,128)S(1)}, f32[1,2,36,432]{3,1,2,0:T(2,128)}, u32[]{:S(2)}) copy-start(f32[1,2,36,432]{3,1,2,0:T(2,128)} %param.9) | copy-start | bytes 373252
  171.1 6.2 %collective-permute-start.5 = (f32[1,8,2304]{2,1,0:T(8,128)S(1)}, f32[1,8,2304]{2,1,0:T(8,128)S(1)}, u32[]{:S(2)}, u32[]{:S(2)}) collective-permute-start(f32[1,8,2304]{2,1,0:T(8,128)S(1)} %slice.465), channel_id=1, source_target_pairs={{16,0},{32,16},{48,32},{64,48},{80,64},{96,80},{112,96},{128,112},... | collective-permute-start | bytes 221192 | tf_op jit(solution)/shard_map/ppermute | solution.py:30
  177.4 15.5 %collective-permute-start.6 = (f32[6,1,2304]{2,1,0:T(1,128)S(1)}, f32[6,1,2304]{2,1,0:T(1,128)S(1)}, u32[]{:S(2)}, u32[]{:S(2)}) collective-permute-start(f32[6,1,2304]{2,1,0:T(1,128)S(1)} %get-tuple-element.69), channel_id=1, source_target_pairs={{0,1},{1,2},{2,3},{3,4},{4,5},{5,6},{6,7},{7,8},{8,9},{9,10},{10,1... | collective-permute-start | bytes 165896 | tf_op jit(solution)/shard_map/ppermute | solution.py:28
  185.7 10.9 %collective-permute-start.7 = (f32[6,1,2304]{2,1,0:T(1,128)S(1)}, f32[6,1,2304]{2,1,0:T(1,128)S(1)}, u32[]{:S(2)}, u32[]{:S(2)}) collective-permute-start(f32[6,1,2304]{2,1,0:T(1,128)S(1)} %get-tuple-element.70), channel_id=1, source_target_pairs={{1,0},{2,1},{3,2},{4,3},{5,4},{6,5},{7,6},{8,7},{9,8},{10,9},{11,1... | collective-permute-start | bytes 165896 | tf_op jit(solution)/shard_map/ppermute | solution.py:30
  208.2 4.3 copy-start.25
  215.7 4.3 copy-start.23
  223.2 4.3 copy-start.21
  238.2 4.4 copy-start.17
  245.7 4.3 copy-start.15
  253.3 4.5 copy-start.13
  259.0 6.4 %copy-start.11 = (f32[36,4,8,64]{3,0,1,2:T(8,128)S(1)}, f32[36,4,8,64]{3,0,1,2:T(8,128)}, u32[]{:S(2)}) copy-start(f32[36,4,8,64]{3,0,1,2:T(8,128)} %get-tuple-element.23) | copy-start | bytes 884740
  268.6 4.4 copy-start.9
  276.1 6.4 %copy-start.7 = (f32[36,4,8,64]{3,0,1,2:T(8,128)S(1)}, f32[36,4,8,64]{3,0,1,2:T(8,128)}, u32[]{:S(2)}) copy-start(f32[36,4,8,64]{3,0,1,2:T(8,128)} %get-tuple-element.27) | copy-start | bytes 884740
  286.1 6.4 %copy-start.4 = (f32[36,4,8,64]{3,0,1,2:T(8,128)S(1)}, f32[36,4,8,64]{3,0,1,2:T(8,128)}, u32[]{:S(2)}) copy-start(f32[36,4,8,64]{3,0,1,2:T(8,128)} %get-tuple-element.29) | copy-start | bytes 884740
  296.2 6.4 %copy-start.1 = (f32[36,4,8,64]{3,0,1,2:T(8,128)S(1)}, f32[36,4,8,64]{3,0,1,2:T(8,128)}, u32[]{:S(2)}) copy-start(f32[36,4,8,64]{3,0,1,2:T(8,128)} %get-tuple-element.31) | copy-start | bytes 884740
  317.0 5.2 copy-start.70
  323.4 189.7 %copy-start.27 = (f32[2,36,12,36]{3,2,0,1:T(8,128)S(1)}, f32[2,36,12,36]{3,2,0,1:T(8,128)}, u32[]{:S(2)}) copy-start(f32[2,36,12,36]{3,2,0,1:T(8,128)} %reshape.331) | copy-start | bytes 373252
  323.4 189.7 %copy-start.28 = (f32[2,36,12,36]{3,2,0,1:T(8,128)S(1)}, f32[2,36,12,36]{3,2,0,1:T(8,128)}, u32[]{:S(2)}) copy-start(f32[2,36,12,36]{3,2,0,1:T(8,128)} %reshape.333) | copy-start | bytes 373252
  515.0 21.3 %all-to-all-start = ((f32[16,2,1,864]{3,2,1,0:T(1,128)}), f32[16,2,1,864]{3,2,1,0:T(1,128)S(1)}, u32[]{:S(2)}, u32[]{:S(2)}) async-start(f32[16,2,1,864]{3,2,1,0:T(1,128)} %stack.2), calls=%async_computation | async-start | bytes 229376 | tf_op jit(solution)/shard_map/all_to_all | solution.py:17
  (55 other events, 103.8 us)
Sparse Core Ops, SparseCore 0:
  32.3 285.0 all-reduce.6
  322.3 189.6 all-reduce.8
